TPU v7x, 32 devices: a whole 2x2x4 slice. The times are simulated.
32 devices in a mesh: segment: 2 (over core), expert: 16 (over z, y, x).
Axes of the slice: x: 2, y: 2, z: 4, core: 2. Of those that a mesh axis runs over, the one named last changes fastest.
Arguments:
- tokens: bfloat16 [2, 1024, 2048], P(None, 'expert'), may hold values from -6 to 6
- routing: int32 [2, 2, 1024, 8], P(None, None, 'expert'), may hold values from 0 to 15, all different within a row; in each aligned block of 64 rows (0 to 63, 64 to 127, ..., all dimensions but the last counted through in order) at most 64 rows name the same one
- norm_gain: bfloat16 [2, 2048], P('segment'), may hold values from 0.5 to 1.5
- router_weight: bfloat16 [2, 2048, 16], P('segment'), may hold values from -0.125 to 0.125
- expert_gate_up: bfloat16 [2, 16, 2048, 768], P('segment', 'expert'), may hold values from -0.125 to 0.125
- expert_down: bfloat16 [2, 16, 384, 2048], P('segment', 'expert'), may hold values from -0.3125 to 0.3125
- pair_index: int32 [64], replicated, may hold values from 0 to 63, each once
- topic_ids: int32 [64], replicated, may hold values from 0 to 7
Outputs:
- final_hidden: bfloat16 [2, 1024, 2048], P('segment', 'expert')
- query_loss: float32 [64], P(('segment', 'expert'))
Inputs may be any that keep to these rules, and one draw needn't show every extreme that they name: `routing`: each row names 8 different experts. In the rows of one device (each aligned block of 64 token rows of one layer and micro-batch) no expert is named by more than 64 rows, a bound that some block reaches. `pair_index`: every passage is the positive of exactly one query.
All inputs are finite; a program needn't handle non-finite values.
Results may differ from a plain program's by a relative error of at most 0.0059.
Values may be sent and summed in bfloat16 or wider, within the bound.
A program may use at most 128 MiB of HBM per device.

v0:
```python
import jax
import jax.numpy as jnp
from jax import lax
from jax.sharding import PartitionSpec as P

SEQ = 16
EPSILON = 1e-06
SOFTMAX_WARMTH = 0.05


def passed_along(block, axis, distance):
    devices = range(lax.axis_size(axis))
    route = [(i - distance, i) for i in devices if i - distance in devices]
    return lax.ppermute(block, axis, route)


def expert_block(received, gate_up, down_proj):
    source_count, slot_count, model_width = received.shape
    flat_rows = received.reshape(source_count * slot_count, model_width)
    projected = jnp.dot(flat_rows, gate_up, preferred_element_type=jnp.float32)
    half_width = gate_up.shape[1] // 2
    hidden = (jax.nn.silu(projected[:, :half_width]) * projected[:, half_width:]).astype(
        jnp.bfloat16
    )
    result = jnp.dot(hidden, down_proj, preferred_element_type=jnp.float32).astype(jnp.bfloat16)
    return result.reshape(source_count, slot_count, model_width)


def moe_layer(inputs, routes, norm_gain, router_weight, gate_up, down_proj):
    row_count, model_width = inputs.shape
    top_count = routes.shape[1]
    expert_count = router_weight.shape[1]
    capacity = 2 * row_count * top_count // expert_count
    widened = inputs.astype(jnp.float32)
    normed = (
        widened
        * lax.rsqrt(jnp.mean(widened * widened, axis=1, keepdims=True) + EPSILON)
        * norm_gain.astype(jnp.float32)
    ).astype(jnp.bfloat16)
    similarity_logits = jnp.dot(normed, router_weight, preferred_element_type=jnp.float32)
    chosen = jnp.take_along_axis(similarity_logits, routes, axis=1)
    raised = jnp.exp(chosen)
    gate_weights = raised / jnp.sum(raised, axis=1, keepdims=True)
    flat_ids = routes.reshape(-1)
    one_hot = (flat_ids[:, None] == jnp.arange(expert_count, dtype=jnp.int32)[None, :]).astype(
        jnp.int32
    )
    earlier = jnp.cumsum(one_hot, axis=0) - one_hot
    slot_index = jnp.sum(earlier * one_hot, axis=1)
    target = flat_ids * capacity + slot_index
    repeated = jnp.repeat(normed, top_count, axis=0)
    outgoing = (
        jnp.zeros((expert_count * capacity, model_width), jnp.bfloat16).at[target].set(repeated)
    )
    outgoing = outgoing.reshape(expert_count, capacity, model_width)
    answered = expert_block(
        lax.all_to_all(outgoing, "expert", split_axis=0, concat_axis=0, tiled=True),
        gate_up,
        down_proj,
    )
    returned = lax.all_to_all(answered, "expert", split_axis=0, concat_axis=0, tiled=True)
    picked = returned.reshape(expert_count * capacity, model_width)[target].astype(jnp.float32)
    picked = picked.reshape(row_count, top_count, model_width)
    mixture = jnp.sum(picked * gate_weights[:, :, None], axis=1)
    return (widened + mixture).astype(jnp.bfloat16)


def pooled_embeddings(final_rows):
    widened = final_rows.astype(jnp.float32)
    pooled = jnp.mean(widened.reshape(-1, SEQ, widened.shape[1]), axis=1)
    return (pooled * lax.rsqrt(jnp.sum(pooled * pooled, axis=1, keepdims=True) + EPSILON)).astype(
        jnp.bfloat16
    )


def local(
    tokens, routing, norm_gain, router_weight, expert_gate_up, expert_down, pair_index, topic_ids
):
    segment_index = lax.axis_index("segment")
    micro_count = tokens.shape[0]
    segment_routes = lax.dynamic_index_in_dim(routing, segment_index, 0, keepdims=False)
    carried = jnp.zeros_like(tokens[0])
    finished = []
    for time_step in range(micro_count + 1):
        fresh_rows = tokens[min(time_step, micro_count - 1)]
        segment_input = jnp.where(segment_index == 0, fresh_rows, carried)
        micro_pick = jnp.clip(time_step - segment_index, 0, micro_count - 1)
        layer_routes = lax.dynamic_index_in_dim(segment_routes, micro_pick, 0, keepdims=False)
        produced = moe_layer(
            segment_input,
            layer_routes,
            norm_gain[0],
            router_weight[0],
            expert_gate_up[0, 0],
            expert_down[0, 0],
        )
        finished.append(produced)
        if time_step < micro_count:
            carried = passed_along(produced, "segment", 1)
    sent_back = passed_along(finished[1], "segment", -1)
    final_rows = jnp.where(segment_index == 0, sent_back, finished[micro_count])
    embedded = pooled_embeddings(final_rows)
    half_count = embedded.shape[0] // 2
    query_vectors = embedded[:half_count]
    passage_vectors = embedded[half_count:]
    device_flat = lax.axis_index(("segment", "expert"))
    columns = jnp.arange(topic_ids.shape[0], dtype=jnp.int32)
    matched = pair_index[:, None] == columns[None, :]
    positive_topic = jnp.sum(
        jnp.where(matched, topic_ids[None, :], jnp.zeros_like(topic_ids)[None, :]), axis=1
    )
    every_query_row = lax.all_gather(query_vectors, ("segment", "expert"), axis=0, tiled=True)
    local_ids = device_flat * half_count + jnp.arange(half_count, dtype=jnp.int32)
    local_topics = lax.dynamic_slice_in_dim(topic_ids, device_flat * half_count, half_count)
    pair_scores = (
        jnp.dot(every_query_row, passage_vectors.T, preferred_element_type=jnp.float32)
        / SOFTMAX_WARMTH
    )
    is_positive = pair_index[:, None] == local_ids[None, :]
    kept_pairs = is_positive | (local_topics[None, :] != positive_topic[:, None])
    partition_part = jnp.sum(
        jnp.where(kept_pairs, jnp.exp(pair_scores), jnp.zeros_like(pair_scores)), axis=1
    )
    positive_part = jnp.sum(
        jnp.where(is_positive, pair_scores, jnp.zeros_like(pair_scores)), axis=1
    )
    partition, positive = (
        lax.psum_scatter(partition_part, ("segment", "expert"), scatter_dimension=0, tiled=True),
        lax.psum_scatter(positive_part, ("segment", "expert"), scatter_dimension=0, tiled=True),
    )
    query_loss = jnp.log(partition) - positive
    return (final_rows[None], query_loss)


def solution(mesh):
    in_specs = (
        P(None, "expert", None),
        P(None, None, "expert", None),
        P("segment", None),
        P("segment", None, None),
        P("segment", "expert", None, None),
        P("segment", "expert", None, None),
        P(),
        P(),
    )
    out_specs = (P("segment", "expert", None), P(("segment", "expert")))
    return jax.shard_map(local, mesh=mesh, in_specs=in_specs, out_specs=out_specs, check_vma=False)
```

profile of v0, /device:TPU:14, one launch (start us, length us, event | category | flops | bytes accessed | tf_op | source)
XLA Modules:
  0.0 794.9 jit_solution(5908741902070264360)
XLA Ops:
  6.5 6.2 scatter_custom_fusion
  12.6 98.8 %all_to_all.30 = bf16[16,64,2048]{2,1,0:T(8,128)(2,1)S(1)} all-to-all(bf16[16,64,2048]{2,1,0:T(8,128)(2,1)} %bitcast.211), channel_id=1, replica_groups=mesh['segment'=2,'expert'=16] {'expert'}, dimensions={0} | all-to-all | bytes 8388608 | tf_op jit(solution)/shard_map/all_to_all | solution.py:57
  114.9 4.3 convolution_convert_fusion.2
  119.2 7.0 all-to-all-start.1
  127.9 3.9 gather_fusion.3
  133.5 84.3 %all-to-all-done.1 = bf16[16,64,2048]{2,1,0:T(8,128)(2,1)} async-done(((bf16[16,64,2048]{2,1,0:T(8,128)(2,1)}), bf16[16,64,2048]{2,1,0:T(8,128)(2,1)}, u32[]{:S(2)}, u32[]{:S(2)}) %all-to-all-start.1) | async-done | bytes 4194336 | tf_op jit(solution)/shard_map/all_to_all | solution.py:61
  217.8 8.0 %gather_fusion = bf16[512,2048]{1,0:T(8,128)(2,1)} fusion(bf16[1024,2048]{1,0:T(8,128)(2,1)} %bitcast.12, s32[1024]{0:T(1024)S(1)} %pad_clamp_fusion.2), kind=kCustom, calls=%fused_computation.3 | custom fusion | bytes 4196352 | tf_op jit(solution)/shard_map/gather | solution.py:62
  235.6 6.2 scatter_custom_fusion.1
  241.7 97.5 %all_to_all.31 = bf16[16,64,2048]{2,1,0:T(8,128)(2,1)S(1)} all-to-all(bf16[16,64,2048]{2,1,0:T(8,128)(2,1)} %bitcast.213), channel_id=1, replica_groups=mesh['segment'=2,'expert'=16] {'expert'}, dimensions={0} | all-to-all | bytes 8388608 | tf_op jit(solution)/shard_map/all_to_all | solution.py:57
  342.7 4.3 convolution_convert_fusion.1
  347.1 6.3 all-to-all-start.3
  357.1 3.9 gather_fusion.4
  361.9 83.8 %all-to-all-done.3 = bf16[16,64,2048]{2,1,0:T(8,128)(2,1)} async-done(((bf16[16,64,2048]{2,1,0:T(8,128)(2,1)}), bf16[16,64,2048]{2,1,0:T(8,128)(2,1)}, u32[]{:S(2)}, u32[]{:S(2)}) %all-to-all-start.3) | async-done | bytes 4194336 | tf_op jit(solution)/shard_map/all_to_all | solution.py:61
  445.7 8.0 %gather_fusion.1 = bf16[512,2048]{1,0:T(8,128)(2,1)} fusion(bf16[1024,2048]{1,0:T(8,128)(2,1)} %bitcast.25, s32[1024]{0:T(1024)S(1)} %pad_clamp_fusion.1), kind=kCustom, calls=%fused_computation.4 | custom fusion | bytes 4196352 | tf_op jit(solution)/shard_map/gather | solution.py:62
  462.7 6.6 scatter_custom_fusion.2
  469.3 97.4 %all_to_all.32 = bf16[16,64,2048]{2,1,0:T(8,128)(2,1)S(1)} all-to-all(bf16[16,64,2048]{2,1,0:T(8,128)(2,1)} %bitcast.212), channel_id=1, replica_groups=mesh['segment'=2,'expert'=16] {'expert'}, dimensions={0} | all-to-all | bytes 8388608 | tf_op jit(solution)/shard_map/all_to_all | solution.py:57
  570.1 4.3 convolution_convert_fusion
  574.5 6.3 all-to-all-start.5
  583.9 3.9 gather_fusion.5
  588.1 85.2 %all-to-all-done.5 = bf16[16,64,2048]{2,1,0:T(8,128)(2,1)} async-done(((bf16[16,64,2048]{2,1,0:T(8,128)(2,1)}), bf16[16,64,2048]{2,1,0:T(8,128)(2,1)}, u32[]{:S(2)}, u32[]{:S(2)}) %all-to-all-start.5) | async-done | bytes 4194336 | tf_op jit(solution)/shard_map/all_to_all | solution.py:61
  673.3 8.0 %gather_fusion.2 = bf16[512,2048]{1,0:T(8,128)(2,1)} fusion(bf16[1024,2048]{1,0:T(8,128)(2,1)} %bitcast.36, s32[1024]{0:T(1024)S(1)} %pad_clamp_fusion), kind=kCustom, calls=%fused_computation.5 | custom fusion | bytes 4196352 | tf_op jit(solution)/shard_map/gather | solution.py:62
  681.3 3.4 fusion
  686.8 57.1 %all-gather = bf16[32,2,2048]{2,1,0:T(2,128)(2,1)S(1)} all-gather(bf16[1,2,2048]{2,1,0:T(2,128)(2,1)S(1)} %slice_bitcast_fusion), channel_id=1, replica_groups=mesh['segment'=2,'expert'=16] {'segment','expert'}, dimensions={0}, use_global_device_ids=true | all-gather | bytes 270336 | tf_op jit(solution)/shard_map/all_gather | solution.py:112
  745.8 48.3 %all-reduce.2 = (f32[64]{0:T(128)S(1)}, f32[64]{0:T(128)S(1)}) all-reduce(f32[64]{0:T(128)S(1)} %get-tuple-element.4, f32[64]{0:T(128)S(1)} %get-tuple-element.3), channel_id=3, replica_groups=mesh['segment'=2,'expert'=16] {'segment','expert'}, use_global_device_ids=true, to_apply=%region_27.29.clone | all-reduce | flops 128 | bytes 1024
  (121 shorter events, 50.5 us)
Async XLA Ops:
  0.6 110.8 %copy-start = (bf16[1,1,2048,768]{3,2,1,0:T(8,128)(2,1)S(1)}, bf16[1,1,2048,768]{3,2,1,0:T(8,128)(2,1)}, u32[]{:S(2)}) copy-start(bf16[1,1,2048,768]{3,2,1,0:T(8,128)(2,1)} %param.14) | copy-start | bytes 9437188
  111.5 3.4 copy-start.5
  119.2 7.4 copy-start.3
  119.2 98.5 %all-to-all-start.1 = ((bf16[16,64,2048]{2,1,0:T(8,128)(2,1)}), bf16[16,64,2048]{2,1,0:T(8,128)(2,1)}, u32[]{:S(2)}, u32[]{:S(2)}) async-start(bf16[16,64,2048]{2,1,0:T(8,128)(2,1)} %bitcast.215), calls=%async_computation.1 | async-start | bytes 8388608 | tf_op jit(solution)/shard_map/all_to_all | solution.py:61
  230.9 2.6 collective-permute-start
  234.7 0.7 copy-start.1
  339.3 3.4 copy-start.6
  347.1 98.6 %all-to-all-start.3 = ((bf16[16,64,2048]{2,1,0:T(8,128)(2,1)}), bf16[16,64,2048]{2,1,0:T(8,128)(2,1)}, u32[]{:S(2)}, u32[]{:S(2)}) async-start(bf16[16,64,2048]{2,1,0:T(8,128)(2,1)} %bitcast.216), calls=%async_computation.3 | async-start | bytes 8388608 | tf_op jit(solution)/shard_map/all_to_all | solution.py:61
  356.9 4.1 copy-start.4
  445.7 11.5 %copy-start.2 = (bf16[64,2048]{1,0:T(8,128)(2,1)S(1)}, bf16[64,2048]{1,0:T(8,128)(2,1)}, u32[]{:S(2)}) copy-start(bf16[64,2048]{1,0:T(8,128)(2,1)} %copy-done.1) | copy-start | bytes 786436
  453.7 6.6 slice-start
  457.9 2.8 collective-permute-start.2
  566.7 3.4 copy-start.7
  574.5 6.5 copy-start.8
  574.5 6.6 copy-start.9
  574.5 98.8 %all-to-all-start.5 = ((bf16[16,64,2048]{2,1,0:T(8,128)(2,1)}), bf16[16,64,2048]{2,1,0:T(8,128)(2,1)}, u32[]{:S(2)}, u32[]{:S(2)}) async-start(bf16[16,64,2048]{2,1,0:T(8,128)(2,1)} %bitcast.214), calls=%async_computation.5 | async-start | bytes 8388608 | tf_op jit(solution)/shard_map/all_to_all | solution.py:61
  581.3 103.5 %collective-permute-start.1 = (bf16[64,2048]{1,0:T(8,128)(2,1)}, bf16[64,2048]{1,0:T(8,128)(2,1)}, u32[]{:S(2)}, u32[]{:S(2)}) collective-permute-start(bf16[64,2048]{1,0:T(8,128)(2,1)} %fusion.45), channel_id=1, source_target_pairs={{16,0},{17,1},{18,2},{19,3},{20,4},{21,5},{22,6},{23,7},{24,8},{25... | collective-permute-start | bytes 786440 | tf_op jit(solution)/shard_map/ppermute | solution.py:14
where the time goes:
time: 804 us; the launch traced here: 795 us
  blocking collectives  399 us (50%)
  waiting for transfers between devices  254 us (32%)
  local copies, waits for them, and re-layouts  60.1 us (7%)
  other arithmetic  28.4 us (4%)
  matrix products  26.9 us (3%)
  starting transfers between devices  24.7 us (3%)
    all_to_all x3, blocking collectives, moe_layer(): lax.all_to_all(outgoing, 'expert', split_axis=0, concat_axis=0, tiled=True)  294 us
    all_to_all x3, waiting for transfers between devices, moe_layer(): lax.all_to_all(answered, 'expert', split_axis=0, concat_axis=0, tiled=True)  253 us
    all_gather x1, blocking collectives, local(): lax.all_gather(query_vectors, ('segment', 'expert'), axis=0, tiled=True)  57.1 us
    unnamed x1, blocking collectives  48.3 us
    gather x3, local copies, waits for them, and re-layouts, moe_layer(): returned.reshape(expert_count * capacity, model_width)[target]  24 us
    all_to_all x3, starting transfers between devices, moe_layer(): lax.all_to_all(answered, 'expert', split_axis=0, concat_axis=0, tiled=True)  19.6 us
    scatter x3, local copies, waits for them, and re-layouts, moe_layer(): jnp.zeros((expert_count * capacity, model_width), jnp.bfloat16).at[target]  18.9 us
  transfers between devices with their start and end apart: 6, of which 5 were waited for; matrix products, arithmetic and copies ran while one was open for 4% of the time, Pallas kernels for 0%

commit v1 on v0

--- a/solution.py
+++ b/solution.py
@@ -6,6 +6,20 @@
 SEQ = 16
 EPSILON = 1e-06
 SOFTMAX_WARMTH = 0.05
+
+
+def supply_boxes_in(inp, where_dim, vector):
+    back = inp.shape
+    y_new = inp.reshape(
+        *back[:where_dim], vector, back[where_dim] // vector, *back[where_dim + 1 :]
+    )
+    return jnp.moveaxis(y_new, where_dim, 0)
+
+
+def trace_packet(packet, axis_no):
+    w1 = list(packet.shape[1:])
+    w1[axis_no] *= packet.shape[0]
+    return jnp.moveaxis(packet, 0, axis_no).reshape(w1)
 
 
 def passed_along(block, axis, distance):
@@ -58,7 +72,18 @@
         gate_up,
         down_proj,
     )
-    returned = lax.all_to_all(answered, "expert", split_axis=0, concat_axis=0, tiled=True)
+    ready = lax.axis_size("expert")
+    block_last = lax.axis_index("expert")
+    val, m_next = (ready, block_last)
+    step_out = supply_boxes_in(answered, 0, val)
+    xs_all = [step_out[m_next]]
+    for rr in range(1, val):
+        w_next = step_out[m_next ^ rr]
+        shaped = lax.ppermute(w_next, axis_name="expert", perm=[(k, k ^ rr) for k in range(val)])
+        xs_all.append(shaped)
+    h_now = jnp.stack(xs_all)
+    step_out = h_now[m_next ^ jnp.arange(val)]
+    returned = trace_packet(step_out, 0)
     picked = returned.reshape(expert_count * capacity, model_width)[target].astype(jnp.float32)
     picked = picked.reshape(row_count, top_count, model_width)
     mixture = jnp.sum(picked * gate_weights[:, :, None], axis=1)

time: 804 us -> 876 us (1.090)
  blocking collectives: 399 us -> 105 us
  waiting for transfers between devices: 254 us -> 472 us
  starting transfers between devices: 24.7 us -> 113 us
  local copies, waits for them, and re-layouts: 60.1 us -> 119 us
    all_to_all x3 -> x0, blocking collectives: 294 us -> none  [moe_layer(): lax.all_to_all(outgoing, 'expert', split_axis=0, concat_axis=0, tiled=True)]
    ppermute x0 -> x45, waiting for transfers between devices: none -> 209 us  [moe_layer(): lax.ppermute(w_next, axis_name='expert', perm=[(k, k ^ rr) for k in range...]
    ppermute x0 -> x45, starting transfers between devices: none -> 87.8 us  [moe_layer(): lax.ppermute(w_next, axis_name='expert', perm=[(k, k ^ rr) for k in range...]
    unnamed x22 -> x88, local copies, waits for them, and re-layouts: 1.53 us -> 34.6 us
    gather x0 -> x3, local copies, waits for them, and re-layouts: none -> 15.3 us  [moe_layer(): step_out = h_now[m_next ^ jnp.arange(val)]]
  transfers between devices with their start and end apart: 6 -> 51, of which waited for: 5 -> 36; matrix products, arithmetic and copies ran while one was open for 4% -> 10% of each run, Pallas kernels for 0% -> 0%
where the time goes in v1:
time: 876 us; the launch traced here: 869 us
  waiting for transfers between devices  472 us (54%)
  local copies, waits for them, and re-layouts  119 us (14%)
  starting transfers between devices  113 us (13%)
  blocking collectives  105 us (12%)
  other arithmetic  33.1 us (4%)
  matrix products  26.7 us (3%)
    all_to_all x3, waiting for transfers between devices, moe_layer(): lax.all_to_all(outgoing, 'expert', split_axis=0, concat_axis=0, tiled=True)  261 us
    ppermute x45, waiting for transfers between devices, moe_layer(): lax.ppermute(w_next, axis_name='expert', perm=[(k, k ^ rr) for k in range...  209 us
    ppermute x45, starting transfers between devices, moe_layer(): lax.ppermute(w_next, axis_name='expert', perm=[(k, k ^ rr) for k in range...  87.8 us
    all_gather x1, blocking collectives, local(): lax.all_gather(query_vectors, ('segment', 'expert'), axis=0, tiled=True)  59.8 us
    unnamed x1, blocking collectives  44.7 us
    unnamed x88, local copies, waits for them, and re-layouts  34.6 us
    gather x3, local copies, waits for them, and re-layouts, moe_layer(): returned.reshape(expert_count * capacity, model_width)[target]  24 us
    all_to_all x3, starting transfers between devices, moe_layer(): lax.all_to_all(outgoing, 'expert', split_axis=0, concat_axis=0, tiled=True)  20.2 us
  transfers between devices with their start and end apart: 51, of which 36 were waited for; matrix products, arithmetic and copies ran while one was open for 10% of the time, Pallas kernels for 0%

profile of v1, /device:TPU:14, one launch (start us, length us, event | category | flops | bytes accessed | tf_op | source)
XLA Modules:
  0.0 869.4 jit_solution(2379078438438628869)
XLA Ops:
  13.3 7.9 all-to-all-start
  30.7 84.8 %all-to-all-done = bf16[16,64,2048]{2,1,0:T(8,128)(2,1)} async-done(((bf16[16,64,2048]{2,1,0:T(8,128)(2,1)}), bf16[16,64,2048]{2,1,0:T(8,128)(2,1)}, u32[]{:S(2)}, u32[]{:S(2)}) %all-to-all-start) | async-done | bytes 4194336 | tf_op jit(solution)/shard_map/all_to_all | solution.py:71
  149.9 9.2 %collective-permute-start.9 = (bf16[1,64,2048]{2,1,0:T(8,128)(2,1)}, bf16[1,64,2048]{2,1,0:T(8,128)(2,1)S(1)}, u32[]{:S(2)}, u32[]{:S(2)}) collective-permute-start(bf16[1,64,2048]{2,1,0:T(8,128)(2,1)} %get-tuple-element.56), channel_id=1, source_target_pairs={{0,10},{1,11},{2,8},{3,9},{4,14},{5,15},{6,12},{7,13},{8,2},{9,3},... | collective-permute-start | bytes 786440 | tf_op jit(solution)/shard_map/ppermute | solution.py:82
  169.1 27.4 %collective-permute-done.8 = bf16[1,64,2048]{2,1,0:T(8,128)(2,1)S(1)} collective-permute-done((bf16[1,64,2048]{2,1,0:T(8,128)(2,1)}, bf16[1,64,2048]{2,1,0:T(8,128)(2,1)S(1)}, u32[]{:S(2)}, u32[]{:S(2)}) %collective-permute-start.8) | collective-permute-done | bytes 262176 | tf_op jit(solution)/shard_map/ppermute | solution.py:82
  196.4 8.5 collective-permute-start.13
  206.6 10.5 %collective-permute-done.10 = bf16[1,64,2048]{2,1,0:T(8,128)(2,1)S(1)} collective-permute-done((bf16[1,64,2048]{2,1,0:T(8,128)(2,1)}, bf16[1,64,2048]{2,1,0:T(8,128)(2,1)S(1)}, u32[]{:S(2)}, u32[]{:S(2)}) %collective-permute-start.10) | collective-permute-done | bytes 262176 | tf_op jit(solution)/shard_map/ppermute | solution.py:82
  217.9 7.9 collective-permute-done.11
  229.1 7.8 collective-permute-done.13
  244.4 8.0 gather_fusion.1
  282.5 88.1 %all-to-all-done.1 = bf16[16,64,2048]{2,1,0:T(8,128)(2,1)} async-done(((bf16[16,64,2048]{2,1,0:T(8,128)(2,1)}), bf16[16,64,2048]{2,1,0:T(8,128)(2,1)}, u32[]{:S(2)}, u32[]{:S(2)}) %all-to-all-start.1) | async-done | bytes 4194336 | tf_op jit(solution)/shard_map/all_to_all | solution.py:71
  422.1 22.9 %collective-permute-done.24 = bf16[1,64,2048]{2,1,0:T(8,128)(2,1)S(1)} collective-permute-done((bf16[1,64,2048]{2,1,0:T(8,128)(2,1)}, bf16[1,64,2048]{2,1,0:T(8,128)(2,1)S(1)}, u32[]{:S(2)}, u32[]{:S(2)}) %collective-permute-start.24) | collective-permute-done | bytes 262176 | tf_op jit(solution)/shard_map/ppermute | solution.py:82
  457.0 7.8 collective-permute-done.26
  465.5 10.5 %collective-permute-done.27 = bf16[1,64,2048]{2,1,0:T(8,128)(2,1)S(1)} collective-permute-done((bf16[1,64,2048]{2,1,0:T(8,128)(2,1)}, bf16[1,64,2048]{2,1,0:T(8,128)(2,1)S(1)}, u32[]{:S(2)}, u32[]{:S(2)}) %collective-permute-start.27) | collective-permute-done | bytes 262176 | tf_op jit(solution)/shard_map/ppermute | solution.py:82
  480.6 9.3 %collective-permute-done.29 = bf16[1,64,2048]{2,1,0:T(8,128)(2,1)S(1)} collective-permute-done((bf16[1,64,2048]{2,1,0:T(8,128)(2,1)S(1)}, bf16[1,64,2048]{2,1,0:T(8,128)(2,1)S(1)}, u32[]{:S(2)}, u32[]{:S(2)}) %collective-permute-start.29) | collective-permute-done | bytes 262176 | tf_op jit(solution)/shard_map/ppermute | solution.py:82
  496.5 8.0 gather_fusion.3
  533.2 88.5 %all-to-all-done.2 = bf16[16,64,2048]{2,1,0:T(8,128)(2,1)} async-done(((bf16[16,64,2048]{2,1,0:T(8,128)(2,1)}), bf16[16,64,2048]{2,1,0:T(8,128)(2,1)}, u32[]{:S(2)}, u32[]{:S(2)}) %all-to-all-start.2) | async-done | bytes 4194336 | tf_op jit(solution)/shard_map/all_to_all | solution.py:71
  658.6 7.1 collective-permute-start.42
  671.6 13.7 %collective-permute-done.40 = bf16[1,64,2048]{2,1,0:T(8,128)(2,1)S(1)} collective-permute-done((bf16[1,64,2048]{2,1,0:T(8,128)(2,1)}, bf16[1,64,2048]{2,1,0:T(8,128)(2,1)S(1)}, u32[]{:S(2)}, u32[]{:S(2)}) %collective-permute-start.40) | collective-permute-done | bytes 262176 | tf_op jit(solution)/shard_map/ppermute | solution.py:82
  688.8 7.7 collective-permute-done.41
  700.2 8.3 collective-permute-done.42
  709.3 11.9 %collective-permute-done.43 = bf16[1,64,2048]{2,1,0:T(8,128)(2,1)S(1)} collective-permute-done((bf16[1,64,2048]{2,1,0:T(8,128)(2,1)}, bf16[1,64,2048]{2,1,0:T(8,128)(2,1)S(1)}, u32[]{:S(2)}, u32[]{:S(2)}) %collective-permute-start.43) | collective-permute-done | bytes 262176 | tf_op jit(solution)/shard_map/ppermute | solution.py:82
  748.5 8.0 gather_fusion.5
  761.9 59.8 %all-gather = bf16[32,2,2048]{2,1,0:T(2,128)(2,1)S(1)} all-gather(bf16[1,2,2048]{2,1,0:T(2,128)(2,1)S(1)} %slice_bitcast_fusion), channel_id=1, replica_groups=mesh['segment'=2,'expert'=16] {'segment','expert'}, dimensions={0}, use_global_device_ids=true | all-gather | bytes 270336 | tf_op jit(solution)/shard_map/all_gather | solution.py:137
  823.7 44.7 %all-reduce.2 = (f32[64]{0:T(128)S(1)}, f32[64]{0:T(128)S(1)}) all-reduce(f32[64]{0:T(128)S(1)} %get-tuple-element.4, f32[64]{0:T(128)S(1)} %get-tuple-element.3), channel_id=3, replica_groups=mesh['segment'=2,'expert'=16] {'segment','expert'}, use_global_device_ids=true, to_apply=%region_27.29.clone | all-reduce | flops 128 | bytes 1024
  (286 shorter events, 299.4 us)
Async XLA Ops:
  13.3 102.2 %all-to-all-start = ((bf16[16,64,2048]{2,1,0:T(8,128)(2,1)}), bf16[16,64,2048]{2,1,0:T(8,128)(2,1)}, u32[]{:S(2)}, u32[]{:S(2)}) async-start(bf16[16,64,2048]{2,1,0:T(8,128)(2,1)} %bitcast.399), calls=%async_computation | async-start | bytes 8388608 | tf_op jit(solution)/shard_map/all_to_all | solution.py:71
  148.0 48.5 %collective-permute-start.8 = (bf16[1,64,2048]{2,1,0:T(8,128)(2,1)}, bf16[1,64,2048]{2,1,0:T(8,128)(2,1)S(1)}, u32[]{:S(2)}, u32[]{:S(2)}) collective-permute-start(bf16[1,64,2048]{2,1,0:T(8,128)(2,1)} %get-tuple-element.57), channel_id=1, source_target_pairs={{0,9},{1,8},{2,11},{3,10},{4,13},{5,12},{6,15},{7,14},{8,1},{9,0},... | collective-permute-start | bytes 786440 | tf_op jit(solution)/shard_map/ppermute | solution.py:82
  149.9 56.0 %collective-permute-start.9 = (bf16[1,64,2048]{2,1,0:T(8,128)(2,1)}, bf16[1,64,2048]{2,1,0:T(8,128)(2,1)S(1)}, u32[]{:S(2)}, u32[]{:S(2)}) collective-permute-start(bf16[1,64,2048]{2,1,0:T(8,128)(2,1)} %get-tuple-element.56), channel_id=1, source_target_pairs={{0,10},{1,11},{2,8},{3,9},{4,14},{5,15},{6,12},{7,13},{8,2},{9,3},... | collective-permute-start | bytes 786440 | tf_op jit(solution)/shard_map/ppermute | solution.py:82
  159.8 57.3 %collective-permute-start.10 = (bf16[1,64,2048]{2,1,0:T(8,128)(2,1)}, bf16[1,64,2048]{2,1,0:T(8,128)(2,1)S(1)}, u32[]{:S(2)}, u32[]{:S(2)}) collective-permute-start(bf16[1,64,2048]{2,1,0:T(8,128)(2,1)} %get-tuple-element.55), channel_id=1, source_target_pairs={{0,11},{1,10},{2,9},{3,8},{4,15},{5,14},{6,13},{7,12},{8,3},{9,2},... | collective-permute-start | bytes 786440 | tf_op jit(solution)/shard_map/ppermute | solution.py:82
  167.2 58.6 %collective-permute-start.11 = (bf16[1,64,2048]{2,1,0:T(8,128)(2,1)}, bf16[1,64,2048]{2,1,0:T(8,128)(2,1)S(1)}, u32[]{:S(2)}, u32[]{:S(2)}) collective-permute-start(bf16[1,64,2048]{2,1,0:T(8,128)(2,1)} %get-tuple-element.54), channel_id=1, source_target_pairs={{0,12},{1,13},{2,14},{3,15},{4,8},{5,9},{6,10},{7,11},{8,4},{9,5},... | collective-permute-start | bytes 786440 | tf_op jit(solution)/shard_map/ppermute | solution.py:82
  167.9 60.5 %collective-permute-start.12 = (bf16[1,64,2048]{2,1,0:T(8,128)(2,1)}, bf16[1,64,2048]{2,1,0:T(8,128)(2,1)S(1)}, u32[]{:S(2)}, u32[]{:S(2)}) collective-permute-start(bf16[1,64,2048]{2,1,0:T(8,128)(2,1)} %get-tuple-element.53), channel_id=1, source_target_pairs={{0,13},{1,12},{2,15},{3,14},{4,9},{5,8},{6,11},{7,10},{8,5},{9,4},... | collective-permute-start | bytes 786440 | tf_op jit(solution)/shard_map/ppermute | solution.py:82
  196.4 40.4 %collective-permute-start.13 = (bf16[1,64,2048]{2,1,0:T(8,128)(2,1)S(1)}, bf16[1,64,2048]{2,1,0:T(8,128)(2,1)S(1)}, u32[]{:S(2)}, u32[]{:S(2)}) collective-permute-start(bf16[1,64,2048]{2,1,0:T(8,128)(2,1)S(1)} %copy-done.6), channel_id=1, source_target_pairs={{0,14},{1,15},{2,12},{3,13},{4,10},{5,11},{6,8},{7,9},{8,6},{9,7},... | collective-permute-start | bytes 786440 | tf_op jit(solution)/shard_map/ppermute | solution.py:82
  205.9 32.7 %collective-permute-start.14 = (bf16[1,64,2048]{2,1,0:T(8,128)(2,1)S(1)}, bf16[1,64,2048]{2,1,0:T(8,128)(2,1)S(1)}, u32[]{:S(2)}, u32[]{:S(2)}) collective-permute-start(bf16[1,64,2048]{2,1,0:T(8,128)(2,1)S(1)} %get-tuple-element.51), channel_id=1, source_target_pairs={{0,15},{1,14},{2,13},{3,12},{4,11},{5,10},{6,9},{7,8},{8,7},{9,6},... | collective-permute-start | bytes 786440 | tf_op jit(solution)/shard_map/ppermute | solution.py:82
  268.5 102.1 %all-to-all-start.1 = ((bf16[16,64,2048]{2,1,0:T(8,128)(2,1)}), bf16[16,64,2048]{2,1,0:T(8,128)(2,1)}, u32[]{:S(2)}, u32[]{:S(2)}) async-start(bf16[16,64,2048]{2,1,0:T(8,128)(2,1)} %bitcast.401), calls=%async_computation.1 | async-start | bytes 8388608 | tf_op jit(solution)/shard_map/all_to_all | solution.py:71
  399.4 45.6 %collective-permute-start.24 = (bf16[1,64,2048]{2,1,0:T(8,128)(2,1)}, bf16[1,64,2048]{2,1,0:T(8,128)(2,1)S(1)}, u32[]{:S(2)}, u32[]{:S(2)}) collective-permute-start(bf16[1,64,2048]{2,1,0:T(8,128)(2,1)} %get-tuple-element.41), channel_id=1, source_target_pairs={{0,9},{1,8},{2,11},{3,10},{4,13},{5,12},{6,15},{7,14},{8,1},{9,0},... | collective-permute-start | bytes 786440 | tf_op jit(solution)/shard_map/ppermute | solution.py:82
  402.6 53.7 %collective-permute-start.25 = (bf16[1,64,2048]{2,1,0:T(8,128)(2,1)}, bf16[1,64,2048]{2,1,0:T(8,128)(2,1)S(1)}, u32[]{:S(2)}, u32[]{:S(2)}) collective-permute-start(bf16[1,64,2048]{2,1,0:T(8,128)(2,1)} %get-tuple-element.40), channel_id=1, source_target_pairs={{0,10},{1,11},{2,8},{3,9},{4,14},{5,15},{6,12},{7,13},{8,2},{9,3},... | collective-permute-start | bytes 786440 | tf_op jit(solution)/shard_map/ppermute | solution.py:82
  411.8 53.0 %collective-permute-start.26 = (bf16[1,64,2048]{2,1,0:T(8,128)(2,1)}, bf16[1,64,2048]{2,1,0:T(8,128)(2,1)S(1)}, u32[]{:S(2)}, u32[]{:S(2)}) collective-permute-start(bf16[1,64,2048]{2,1,0:T(8,128)(2,1)} %get-tuple-element.39), channel_id=1, source_target_pairs={{0,11},{1,10},{2,9},{3,8},{4,15},{5,14},{6,13},{7,12},{8,3},{9,2},... | collective-permute-start | bytes 786440 | tf_op jit(solution)/shard_map/ppermute | solution.py:82
  419.4 56.6 %collective-permute-start.27 = (bf16[1,64,2048]{2,1,0:T(8,128)(2,1)}, bf16[1,64,2048]{2,1,0:T(8,128)(2,1)S(1)}, u32[]{:S(2)}, u32[]{:S(2)}) collective-permute-start(bf16[1,64,2048]{2,1,0:T(8,128)(2,1)} %get-tuple-element.38), channel_id=1, source_target_pairs={{0,12},{1,13},{2,14},{3,15},{4,8},{5,9},{6,10},{7,11},{8,4},{9,5},... | collective-permute-start | bytes 786440 | tf_op jit(solution)/shard_map/ppermute | solution.py:82
  420.1 59.8 %collective-permute-start.28 = (bf16[1,64,2048]{2,1,0:T(8,128)(2,1)}, bf16[1,64,2048]{2,1,0:T(8,128)(2,1)S(1)}, u32[]{:S(2)}, u32[]{:S(2)}) collective-permute-start(bf16[1,64,2048]{2,1,0:T(8,128)(2,1)} %get-tuple-element.37), channel_id=1, source_target_pairs={{0,13},{1,12},{2,15},{3,14},{4,9},{5,8},{6,11},{7,10},{8,5},{9,4},... | collective-permute-start | bytes 786440 | tf_op jit(solution)/shard_map/ppermute | solution.py:82
  445.0 44.9 %collective-permute-start.29 = (bf16[1,64,2048]{2,1,0:T(8,128)(2,1)S(1)}, bf16[1,64,2048]{2,1,0:T(8,128)(2,1)S(1)}, u32[]{:S(2)}, u32[]{:S(2)}) collective-permute-start(bf16[1,64,2048]{2,1,0:T(8,128)(2,1)S(1)} %copy-done.7), channel_id=1, source_target_pairs={{0,14},{1,15},{2,12},{3,13},{4,10},{5,11},{6,8},{7,9},{8,6},{9,7},... | collective-permute-start | bytes 786440 | tf_op jit(solution)/shard_map/ppermute | solution.py:82
  456.2 34.4 %collective-permute-start.30 = (bf16[1,64,2048]{2,1,0:T(8,128)(2,1)S(1)}, bf16[1,64,2048]{2,1,0:T(8,128)(2,1)S(1)}, u32[]{:S(2)}, u32[]{:S(2)}) collective-permute-start(bf16[1,64,2048]{2,1,0:T(8,128)(2,1)S(1)} %get-tuple-element.35), channel_id=1, source_target_pairs={{0,15},{1,14},{2,13},{3,12},{4,11},{5,10},{6,9},{7,8},{8,7},{9,6},... | collective-permute-start | bytes 786440 | tf_op jit(solution)/shard_map/ppermute | solution.py:82
  520.2 101.6 %all-to-all-start.2 = ((bf16[16,64,2048]{2,1,0:T(8,128)(2,1)}), bf16[16,64,2048]{2,1,0:T(8,128)(2,1)}, u32[]{:S(2)}, u32[]{:S(2)}) async-start(bf16[16,64,2048]{2,1,0:T(8,128)(2,1)} %bitcast.400), calls=%async_computation.2 | async-start | bytes 8388608 | tf_op jit(solution)/shard_map/all_to_all | solution.py:71
  526.8 233.2 %collective-permute-start.31 = (bf16[64,2048]{1,0:T(8,128)(2,1)}, bf16[64,2048]{1,0:T(8,128)(2,1)}, u32[]{:S(2)}, u32[]{:S(2)}) collective-permute-start(bf16[64,2048]{1,0:T(8,128)(2,1)} %fusion.45), channel_id=1, source_target_pairs={{16,0},{17,1},{18,2},{19,3},{20,4},{21,5},{22,6},{23,7},{24,8},{25... | collective-permute-start | bytes 786440 | tf_op jit(solution)/shard_map/ppermute | solution.py:28
  650.7 34.6 %collective-permute-start.40 = (bf16[1,64,2048]{2,1,0:T(8,128)(2,1)}, bf16[1,64,2048]{2,1,0:T(8,128)(2,1)S(1)}, u32[]{:S(2)}, u32[]{:S(2)}) collective-permute-start(bf16[1,64,2048]{2,1,0:T(8,128)(2,1)} %get-tuple-element.26), channel_id=1, source_target_pairs={{0,8},{1,9},{2,10},{3,11},{4,12},{5,13},{6,14},{7,15},{8,0},{9,1},... | collective-permute-start | bytes 786440 | tf_op jit(solution)/shard_map/ppermute | solution.py:82
  654.4 42.1 %collective-permute-start.41 = (bf16[1,64,2048]{2,1,0:T(8,128)(2,1)}, bf16[1,64,2048]{2,1,0:T(8,128)(2,1)S(1)}, u32[]{:S(2)}, u32[]{:S(2)}) collective-permute-start(bf16[1,64,2048]{2,1,0:T(8,128)(2,1)} %get-tuple-element.25), channel_id=1, source_target_pairs={{0,9},{1,8},{2,11},{3,10},{4,13},{5,12},{6,15},{7,14},{8,1},{9,0},... | collective-permute-start | bytes 786440 | tf_op jit(solution)/shard_map/ppermute | solution.py:82
  658.6 49.9 %collective-permute-start.42 = (bf16[1,64,2048]{2,1,0:T(8,128)(2,1)}, bf16[1,64,2048]{2,1,0:T(8,128)(2,1)S(1)}, u32[]{:S(2)}, u32[]{:S(2)}) collective-permute-start(bf16[1,64,2048]{2,1,0:T(8,128)(2,1)} %get-tuple-element.24), channel_id=1, source_target_pairs={{0,10},{1,11},{2,8},{3,9},{4,14},{5,15},{6,12},{7,13},{8,2},{9,3},... | collective-permute-start | bytes 786440 | tf_op jit(solution)/shard_map/ppermute | solution.py:82
  666.4 54.7 %collective-permute-start.43 = (bf16[1,64,2048]{2,1,0:T(8,128)(2,1)}, bf16[1,64,2048]{2,1,0:T(8,128)(2,1)S(1)}, u32[]{:S(2)}, u32[]{:S(2)}) collective-permute-start(bf16[1,64,2048]{2,1,0:T(8,128)(2,1)} %get-tuple-element.23), channel_id=1, source_target_pairs={{0,11},{1,10},{2,9},{3,8},{4,15},{5,14},{6,13},{7,12},{8,3},{9,2},... | collective-permute-start | bytes 786440 | tf_op jit(solution)/shard_map/ppermute | solution.py:82
  685.3 43.5 %collective-permute-start.44 = (bf16[1,64,2048]{2,1,0:T(8,128)(2,1)}, bf16[1,64,2048]{2,1,0:T(8,128)(2,1)S(1)}, u32[]{:S(2)}, u32[]{:S(2)}) collective-permute-start(bf16[1,64,2048]{2,1,0:T(8,128)(2,1)} %get-tuple-element.22), channel_id=1, source_target_pairs={{0,12},{1,13},{2,14},{3,15},{4,8},{5,9},{6,10},{7,11},{8,4},{9,5},... | collective-permute-start | bytes 786440 | tf_op jit(solution)/shard_map/ppermute | solution.py:82
  696.5 39.9 %collective-permute-start.45 = (bf16[1,64,2048]{2,1,0:T(8,128)(2,1)S(1)}, bf16[1,64,2048]{2,1,0:T(8,128)(2,1)S(1)}, u32[]{:S(2)}, u32[]{:S(2)}) collective-permute-start(bf16[1,64,2048]{2,1,0:T(8,128)(2,1)S(1)} %copy-done.5), channel_id=1, source_target_pairs={{0,13},{1,12},{2,15},{3,14},{4,9},{5,8},{6,11},{7,10},{8,5},{9,4},... | collective-permute-start | bytes 786440 | tf_op jit(solution)/shard_map/ppermute | solution.py:82
  (51 other events, 1064.5 us)
